TPU v7x, 32 devices: a whole 2x2x4 slice. The times are simulated.
32 devices in a mesh: groups: 2 (over x), fsdp: 16 (over z, y, core).
Axes of the slice: x: 2, y: 2, z: 4, core: 2. Of those that a mesh axis runs over, the one named last changes fastest.
Arguments:
- inputs: bfloat16 [4096, 4096], P(('groups', 'fsdp')), parts along dimension 0, may hold values from -6 to 6
- cotangent: bfloat16 [4096, 4096], P(('groups', 'fsdp')), parts along dimension 0, may hold values from -6 to 6
- tile_store: bfloat16 [256, 128, 128], P('fsdp'), may hold values from -0.5 to 0.5
- pattern: int32 [2, 40], replicated, may hold values from 0 to 111, as said below
- tile_slot: int32 [3, 40], replicated, may hold values from 0 to 255, as said below
Outputs:
- output: bfloat16 [4096, 4096], P(('groups', 'fsdp')), parts along dimension 0
- input_grad: bfloat16 [4096, 4096], P(('groups', 'fsdp')), parts along dimension 0
- tile_grads: float32 [512, 128, 128], P(('groups', 'fsdp')), parts along dimension 0
There are 2 independent parts, one for each index of `groups`. A program takes and returns all parts, laid end to end along the dimension named above; an argument that names none is the same for every part. Nothing has to cross between parts.
Inputs may be any that keep to these rules, and one draw needn't show every extreme that they name: The 40 pairs (pattern[0, j], pattern[1, j]) are distinct; pattern[0] lies below 32, pattern[1] below 112. `tile_slot`: all 120 entries are distinct. Slot s belongs to device s // 16 of fsdp; at least one device holds tiles in all of its 16 slots.
All inputs are finite; a program needn't handle non-finite values.
Results may differ from a plain program's by a relative error of at most 0.0049.
Values may be sent and summed in bfloat16 or wider, within the bound.
A program may use at most 128 MiB of HBM per device.

v0:
```python
import jax
import jax.numpy as jnp
from jax import lax
from jax.sharding import PartitionSpec as P

FF = 14336


def project_pair(tok_tiles, w_gate, w_up, col_index, col_blocks):
    gate = jax.ops.segment_sum(
        jnp.einsum("tjd,jdf->jtf", tok_tiles, w_gate, preferred_element_type=jnp.float32),
        col_index,
        num_segments=col_blocks,
    )
    up = jax.ops.segment_sum(
        jnp.einsum("tjd,jdf->jtf", tok_tiles, w_up, preferred_element_type=jnp.float32),
        col_index,
        num_segments=col_blocks,
    )
    return (gate, up)


def on_device(inputs, cotangent, tile_store, pattern, tile_slot):
    n_rows, width = inputs.shape
    side = tile_store.shape[1]
    row_blocks = width // side
    col_blocks = FF // side
    row_index = pattern[0]
    col_index = pattern[1]
    flat_slots = tile_slot.reshape(-1)
    gathered = lax.all_gather(tile_store, "fsdp", axis=0, tiled=True)
    w_gate = jnp.take(gathered, tile_slot[0], axis=0)
    w_up = jnp.take(gathered, tile_slot[1], axis=0)
    w_down = jnp.take(gathered, tile_slot[2], axis=0)
    tok_tiles = jnp.take(inputs.reshape(n_rows, row_blocks, side), row_index, axis=1)
    cot_tiles = jnp.take(cotangent.reshape(n_rows, row_blocks, side), row_index, axis=1)
    gate, up = project_pair(tok_tiles, w_gate, w_up, col_index, col_blocks)
    hidden = (jax.nn.silu(gate) * up).astype(jnp.bfloat16)
    hidden_tiles = hidden[col_index]
    output = jax.ops.segment_sum(
        jnp.einsum("jtf,jfd->jtd", hidden_tiles, w_down, preferred_element_type=jnp.float32),
        row_index,
        num_segments=row_blocks,
    )
    output = output.transpose(1, 0, 2).reshape(n_rows, width).astype(jnp.bfloat16)
    d_hidden = jax.ops.segment_sum(
        jnp.einsum("tjd,jfd->jtf", cot_tiles, w_down, preferred_element_type=jnp.float32),
        col_index,
        num_segments=col_blocks,
    )
    sigmoid_gate = jax.nn.sigmoid(gate)
    activated = gate * sigmoid_gate
    d_gate = (d_hidden * up * sigmoid_gate * (1.0 + gate * (1.0 - sigmoid_gate))).astype(
        jnp.bfloat16
    )
    d_up = (d_hidden * activated).astype(jnp.bfloat16)
    gate_tiles = d_gate[col_index]
    up_tiles = d_up[col_index]
    back = jnp.einsum("jtf,jdf->jtd", gate_tiles, w_gate, preferred_element_type=jnp.float32)
    back = back + jnp.einsum("jtf,jdf->jtd", up_tiles, w_up, preferred_element_type=jnp.float32)
    input_grad = jax.ops.segment_sum(back, row_index, num_segments=row_blocks)
    input_grad = input_grad.transpose(1, 0, 2).reshape(n_rows, width).astype(jnp.bfloat16)
    grad_gate = jnp.einsum(
        "tjd,jtf->jdf", tok_tiles, gate_tiles, preferred_element_type=jnp.float32
    )
    grad_up = jnp.einsum("tjd,jtf->jdf", tok_tiles, up_tiles, preferred_element_type=jnp.float32)
    grad_down = jnp.einsum(
        "jtf,tjd->jfd", hidden_tiles, cot_tiles, preferred_element_type=jnp.float32
    )
    grads = jnp.concatenate([grad_gate, grad_up, grad_down], axis=0)
    grid = jnp.zeros((gathered.shape[0], side, side), jnp.float32).at[flat_slots].set(grads)
    tile_grads = lax.psum_scatter(grid, "fsdp", scatter_dimension=0, tiled=True)
    return (output, input_grad, tile_grads)


def solution(mesh):
    placed = (
        P(("groups", "fsdp"), None),
        P(("groups", "fsdp"), None),
        P("fsdp", None, None),
        P(),
        P(),
    )
    return jax.shard_map(
        on_device,
        mesh=mesh,
        in_specs=placed,
        out_specs=(
            P(("groups", "fsdp"), None),
            P(("groups", "fsdp"), None),
            P(("groups", "fsdp"), None, None),
        ),
        check_vma=False,
    )
```

profile of v0, /device:TPU:0, one launch (start us, length us, event | category | flops | bytes accessed | tf_op | source)
XLA Modules:
  0.0 403.5 jit_solution(5974833091071041052)
XLA Ops:
  15.8 71.9 %all-gather.2.cloned.1.call-done = bf16[256,128,128]{2,1,0:T(8,128)(2,1)} async-done(((bf16[16,128,128]{2,1,0:T(8,128)(2,1)}), bf16[256,128,128]{2,1,0:T(8,128)(2,1)}) %all-gather.2.cloned.1.call-update) | async-done | bytes 8388624 | tf_op jit(solution)/shard_map/all_gather | solution.py:31
  87.8 5.2 %gather_fusion.6 = bf16[40,128,128]{2,1,0:T(8,128)(2,1)} fusion(bf16[256,128,128]{2,1,0:T(8,128)(2,1)} %all-gather.2.cloned.1.call-done, s32[1024]{0:T(1024)S(1)} %get-tuple-element.28), kind=kCustom, calls=%fused_computation.4.clone | custom fusion | bytes 2621600 | tf_op jit(solution)/shard_map/jit(_take)/gather | solution.py:34
  93.0 3.9 fusion.3
  96.9 3.9 broadcast.50.clone
  100.8 10.1 %scatter_fusion.3 = f32[112,128,128]{2,1,0:T(8,128)} fusion(f32[112,128,128]{2,1,0:T(8,128)} %broadcast.50.clone, s32[40]{0:T(128)S(1)} %get-tuple-element.26, f32[40,128,128]{2,1,0:T(8,128)} %fusion.3), kind=kCustom, calls=%fused_computation.11 | custom fusion | flops 655360 | bytes 7864480 | tf_op jit(solution)/shard_map/scatter-add | solution.py:46
  111.0 5.3 %gather_fusion.4 = bf16[40,128,128]{2,1,0:T(8,128)(2,1)} fusion(bf16[256,128,128]{2,1,0:T(8,128)(2,1)} %all-gather.2.cloned.1.call-done, s32[1024]{0:T(1024)S(1)} %pad_clamp_fusion.3), kind=kCustom, calls=%fused_computation.1.clone | custom fusion | bytes 2621600 | tf_op jit(solution)/shard_map/jit(_take)/gather | solution.py:32
  116.2 3.4 fusion.11
  119.7 3.9 broadcast.50.clone.1
  123.6 10.0 %scatter_fusion = f32[112,128,128]{2,1,0:T(8,128)} fusion(f32[112,128,128]{2,1,0:T(8,128)} %broadcast.50.clone.1, s32[40]{0:T(128)S(1)} %get-tuple-element.26, f32[40,128,128]{2,1,0:T(8,128)} %fusion.11), kind=kCustom, calls=%fused_computation.8 | custom fusion | flops 655360 | bytes 7864480 | tf_op jit(solution)/shard_map/scatter-add | solution.py:10
  133.5 5.2 %gather_fusion.5 = bf16[40,128,128]{2,1,0:T(8,128)(2,1)} fusion(bf16[256,128,128]{2,1,0:T(8,128)(2,1)} %all-gather.2.cloned.1.call-done, s32[1024]{0:T(1024)S(1)} %get-tuple-element.29), kind=kCustom, calls=%fused_computation.3.clone | custom fusion | bytes 2621600 | tf_op jit(solution)/shard_map/jit(_take)/gather | solution.py:33
  138.8 3.4 fusion.9
  142.2 3.9 broadcast.50.clone.2
  146.1 10.0 %scatter_fusion.1 = f32[112,128,128]{2,1,0:T(8,128)} fusion(f32[112,128,128]{2,1,0:T(8,128)} %broadcast.50.clone.2, s32[40]{0:T(128)S(1)} %get-tuple-element.26, f32[40,128,128]{2,1,0:T(8,128)} %fusion.9), kind=kCustom, calls=%fused_computation.9 | custom fusion | flops 655360 | bytes 7864480 | tf_op jit(solution)/shard_map/scatter-add | solution.py:15
  156.1 13.1 %multiply_convert_fusion = (bf16[112,128,128]{2,1,0:T(8,128)(2,1)}, bf16[112,128,128]{2,1,0:T(8,128)(2,1)}, bf16[112,128,128]{2,1,0:T(8,128)(2,1)}) fusion(f32[112,128,128]{2,1,0:T(8,128)} %scatter_fusion.3, f32[112,128,128]{2,1,0:T(8,128)} %scatter_fusion, f32[112,128,128]{2,1,0:T(8,128)} %scatter_fusion.1), kind=kLoop, calls=%fused_computation.15 | loop fusion | flops 27525120 | bytes 33030144 | tf_op jit(solution)/shard_map/convert_element_type | solution.py:56
  169.2 3.9 gather_fusion
  173.2 3.9 gather_fusion.1
  177.0 3.9 gather_fusion.2
  185.0 3.5 pad_maximum_fusion
  188.6 7.9 %broadcast_in_dim.25 = f32[256,128,128]{2,1,0:T(8,128)} broadcast(f32[]{:T(128)} %constant.21.clone.1), dimensions={} | broadcast | bytes 16777220 | tf_op jit(solution)/shard_map/broadcast_in_dim | solution.py:71
  196.4 23.3 %scatter_fusion.5 = f32[256,128,128]{2,1,0:T(8,128)} fusion(f32[256,128,128]{2,1,0:T(8,128)} %broadcast_in_dim.25, s32[120]{0:T(128)S(1)} %fusion.16, f32[120,128,128]{2,1,0:T(8,128)} %pad_maximum_fusion), kind=kCustom, calls=%fused_computation.13 | custom fusion | bytes 23593440 | tf_op jit(solution)/shard_map/scatter | solution.py:71
  221.0 3.4 fusion.14
  224.7 7.2 %scatter_fusion.2 = f32[32,128,128]{2,1,0:T(8,128)S(1)} fusion(f32[32,128,128]{2,1,0:T(8,128)S(1)} %broadcast.49.clone, s32[40]{0:T(128)S(1)} %get-tuple-element.27, f32[40,128,128]{2,1,0:T(8,128)} %fusion.14), kind=kCustom, calls=%fused_computation.10 | custom fusion | flops 655360 | bytes 7864480 | tf_op jit(solution)/shard_map/scatter-add | solution.py:40
  243.0 6.8 %scatter_fusion.4 = f32[32,128,128]{2,1,0:T(8,128)S(1)} fusion(f32[32,128,128]{2,1,0:T(8,128)S(1)} %broadcast.49.clone.1, s32[40]{0:T(128)S(1)} %get-tuple-element.27, f32[40,128,128]{2,1,0:T(8,128)} %convolution_add_fusion), kind=kCustom, calls=%fused_computation.12 | custom fusion | flops 655360 | bytes 7864480 | tf_op jit(solution)/shard_map/scatter-add | solution.py:61
  251.9 144.7 %reduce-scatter.2.cloned.1.call-done = f32[16,128,128]{2,1,0:T(8,128)} async-done(((f32[256,128,128]{2,1,0:T(8,128)}), f32[16,128,128]{2,1,0:T(8,128)}) %reduce-scatter.2.cloned.1.call-update) | async-done | bytes 1048592 | tf_op jit(solution)/shard_map/reduce_scatter | solution.py:72
  (51 shorter events, 27.3 us)
Async XLA Ops:
  7.2 80.6 %all-gather.2.cloned.1.call-start = ((), (), s32[]{:S(2)}) async-start(), calls=%async_computation.1 | async-start | bytes 8912896 | tf_op jit(solution)/shard_map/all_gather | solution.py:31
  7.9 388.8 %reduce-scatter.2.cloned.1.call-start = ((), (), s32[]{:S(2)}) async-start(), calls=%async_computation.2 | async-start | bytes 17825792 | tf_op jit(solution)/shard_map/reduce_scatter | solution.py:72
  9.6 1.2 copy-start.6
  11.5 1.3 copy-start.8
  13.6 2.0 copy-start.7
  181.0 2.1 copy-start.3
  183.1 1.3 copy-start.5
  219.7 1.3 copy-start.2
  235.5 2.4 copy-start
  237.9 1.6 copy-start.1
  237.9 2.2 copy-start.4
Sparse Core Ops, SparseCore 0:
  10.2 77.5 all-gather.1
  219.9 176.7 reduce-scatter.1
where the time goes:
time: 405 us; the launch traced here: 404 us
  waiting for transfers between devices  217 us (54%)
  local copies, waits for them, and re-layouts  88.4 us (22%)
  other arithmetic  62.1 us (15%)
  matrix products  21.3 us (5%)
  between operations  14.3 us (4%)
    reduce_scatter x1, waiting for transfers between devices, on_device(): tile_grads = lax.psum_scatter(grid, 'fsdp', scatter_dimension=0, tiled=True)  145 us
    all_gather x1, waiting for transfers between devices, on_device(): gathered = lax.all_gather(tile_store, 'fsdp', axis=0, tiled=True)  71.9 us
    scatter x1, local copies, waits for them, and re-layouts, on_device(): jnp.zeros((gathered.shape[0], side, side), jnp.float32).at[flat_slots]  23.3 us
    convert_element_type x1, other arithmetic, on_device(): d_up = (d_hidden * activated).astype(jnp.bfloat16)  13.1 us
    another operation x5, local copies, waits for them, and re-layouts  12.2 us
    scatter-add x1, other arithmetic, on_device(): jax.ops.segment_sum(jnp.einsum('tjd,jfd->jtf', cot_tiles, w_down, preferr...  10.1 us
    scatter-add x1, other arithmetic, project_pair(): jax.ops.segment_sum(jnp.einsum('tjd,jdf->jtf', tok_tiles, w_up, preferred...  10 us
    scatter-add x1, other arithmetic, project_pair(): jax.ops.segment_sum(jnp.einsum('tjd,jdf->jtf', tok_tiles, w_gate, preferr...  9.96 us
  transfers between devices with their start and end apart: 2, of which 2 were waited for; matrix products, arithmetic and copies ran while one was open for 9% of the time, Pallas kernels for 0%

commit v1 on v0

v1 whole, which is shorter than its diff:
```python
import jax
import jax.numpy as jnp
from jax import lax
from jax.experimental import pallas as pl
from jax.experimental.pallas import tpu as pltpu
from jax.sharding import PartitionSpec as P

BF = jnp.bfloat16
F32 = jnp.float32
VMEM_BYTES = 56 * 1024 * 1024


def dot(a, b, ca, cb):
    return lax.dot_general(a, b, (((ca,), (cb,)), ((), ())), preferred_element_type=F32)


def layer_kernel(
    idx, x, c, store, out, xgrad, grads,
    wgu, wd, gu, dh, hid, dgu, oacc, xacc, sems,
):
    tiles = wd.shape[0]
    side = wd.shape[1]
    row_blocks = oacc.shape[0]

    def fetch(j, carry):
        pltpu.make_async_copy(store.at[idx[2, j]], wgu.at[0, j], sems.at[0]).start()
        pltpu.make_async_copy(store.at[idx[3, j]], wgu.at[1, j], sems.at[0]).start()
        pltpu.make_async_copy(store.at[idx[4, j]], wd.at[j], sems.at[1]).start()
        return carry

    lax.fori_loop(0, tiles, fetch, 0)

    def clear(s, carry):
        grads[s] = jnp.zeros((side, side), BF)
        return carry

    lax.fori_loop(0, grads.shape[0], clear, 0, unroll=8)

    def clear_rows(s, carry):
        oacc[s] = jnp.zeros((side, side), F32)
        xacc[s] = jnp.zeros((side, side), F32)
        return carry

    lax.fori_loop(0, row_blocks, clear_rows, 0, unroll=4)
    pltpu.make_async_copy(wgu, wgu, sems.at[0]).wait()
    pltpu.make_async_copy(wd, wd, sems.at[1]).wait()

    def block(ref, j):
        return ref[:, pl.ds(pl.multiple_of(idx[0, j] * side, side), side)]

    def forward(j, carry):
        k = idx[1, j]
        xj = block(x, j)
        w2 = jnp.concatenate([wgu[0, j], wgu[1, j]], axis=1)
        part = dot(xj, w2, 1, 0)
        dpart = dot(block(c, j), wd[j], 1, 1)
        keep = k != j
        gu[k] = jnp.where(keep, gu[k], 0.0) + part
        dh[k] = jnp.where(keep, dh[k], 0.0) + dpart
        return carry

    lax.fori_loop(0, tiles, forward, 0, unroll=4)

    def gates(j, carry):
        @pl.when(idx[1, j] == j)
        def _():
            gate = gu[j, :, :side]
            up = gu[j, :, side:]
            d = dh[j]
            sig = jax.nn.sigmoid(gate)
            act = gate * sig
            hid[j] = (act * up).astype(BF)
            dgu[j, :, :side] = (d * up * sig * (1.0 + gate * (1.0 - sig))).astype(BF)
            dgu[j, :, side:] = (d * act).astype(BF)

        return carry

    lax.fori_loop(0, tiles, gates, 0)

    def backward(j, carry):
        a = idx[0, j]
        k = idx[1, j]
        h = hid[k]
        d2 = dgu[k]
        xj = block(x, j)
        cj = block(c, j)
        w2 = jnp.concatenate([wgu[0, j], wgu[1, j]], axis=1)
        oacc[a] += dot(h, wd[j], 1, 0)
        xacc[a] += dot(d2, w2, 1, 1)
        g2 = dot(xj, d2, 0, 0).astype(BF)
        grads[idx[2, j]] = g2[:, :side]
        grads[idx[3, j]] = g2[:, side:]
        grads[idx[4, j]] = dot(h, cj, 0, 0).astype(BF)
        return carry

    lax.fori_loop(0, tiles, backward, 0, unroll=4)

    for s in range(row_blocks):
        out[:, s * side:(s + 1) * side] = oacc[s].astype(BF)
        xgrad[:, s * side:(s + 1) * side] = xacc[s].astype(BF)


def layer(idx, x, c, store):
    n_rows, width = x.shape
    slots, side, _ = store.shape
    tiles = idx.shape[1]
    row_blocks = width // side
    vmem = pl.BlockSpec(memory_space=pltpu.VMEM)
    return pl.pallas_call(
        layer_kernel,
        out_shape=(
            jax.ShapeDtypeStruct(x.shape, BF),
            jax.ShapeDtypeStruct(x.shape, BF),
            jax.ShapeDtypeStruct(store.shape, BF),
        ),
        in_specs=[pl.BlockSpec(memory_space=pltpu.SMEM), vmem, vmem, pl.BlockSpec(memory_space=pl.ANY)],
        out_specs=(vmem, vmem, vmem),
        scratch_shapes=[
            pltpu.VMEM((2, tiles, side, side), BF),
            pltpu.VMEM((tiles, side, side), BF),
            pltpu.VMEM((tiles, n_rows, 2 * side), F32),
            pltpu.VMEM((tiles, n_rows, side), F32),
            pltpu.VMEM((tiles, n_rows, side), BF),
            pltpu.VMEM((tiles, n_rows, 2 * side), BF),
            pltpu.VMEM((row_blocks, n_rows, side), F32),
            pltpu.VMEM((row_blocks, n_rows, side), F32),
            pltpu.SemaphoreType.DMA((2,)),
        ],
        compiler_params=pltpu.CompilerParams(vmem_limit_bytes=VMEM_BYTES),
    )(idx, x, c, store)


def on_device(inputs, cotangent, tile_store, pattern, tile_slot):
    cols = pattern[1]
    first = jnp.argmax(cols[:, None] == cols[None, :], axis=1).astype(jnp.int32)
    idx = jnp.concatenate([pattern[:1], first[None], tile_slot], axis=0)
    gathered = lax.all_gather(tile_store, "fsdp", axis=0, tiled=True)
    output, input_grad, grads = layer(idx, inputs, cotangent, gathered)
    tile_grads = lax.psum_scatter(grads, "fsdp", scatter_dimension=0, tiled=True)
    return output, input_grad, tile_grads.astype(F32)


def solution(mesh):
    placed = (
        P(("groups", "fsdp"), None),
        P(("groups", "fsdp"), None),
        P("fsdp", None, None),
        P(),
        P(),
    )
    return jax.shard_map(
        on_device,
        mesh=mesh,
        in_specs=placed,
        out_specs=(
            P(("groups", "fsdp"), None),
            P(("groups", "fsdp"), None),
            P(("groups", "fsdp"), None, None),
        ),
        check_vma=False,
    )
```

time: 405 us -> 217 us (0.54)
  local copies, waits for them, and re-layouts: 88.4 us -> 0.76 us
  other arithmetic: 62.1 us -> 4.1 us
  waiting for transfers between devices: 217 us -> 181 us
  matrix products: 21.3 us -> 0 us
  Pallas kernels: 0 us -> 16.9 us
    scatter-add x5 -> x0, other arithmetic: 44.1 us -> none  [the longest x1 10.1 us: on_device(): jax.ops.segment_sum(jnp.einsum('tjd,jfd->jtf', cot_tiles, w_down, preferr...]
    reduce_scatter x1, waiting for transfers between devices: 145 us -> 103 us  [on_device(): lax.psum_scatter(grads, 'fsdp', scatter_dimension=0, tiled=True)]
    gather x8 -> x0, local copies, waits for them, and re-layouts: 30.3 us -> none  [the longest x1 5.26 us: on_device(): w_gate = jnp.take(gathered, tile_slot[0], axis=0)]
    scatter x1 -> x0, local copies, waits for them, and re-layouts: 23.3 us -> none  [on_device(): jnp.zeros((gathered.shape[0], side, side), jnp.float32).at[flat_slots]]
    dot_general x9 -> x0, matrix products: 21.3 us -> none  [the longest x1 3.89 us: on_device(): jnp.einsum('tjd,jfd->jtf', cot_tiles, w_down, preferred_element_type=jnp....]
    pallas_call x0 -> x1, Pallas kernels: none -> 16.9 us  [layer(): pl.pallas_call(layer_kernel, out_shape=(jax.ShapeDtypeStruct(x.shape, BF)...]
    convert_element_type x3 -> x1, other arithmetic: 14.4 us -> 2.12 us  [on_device(): return (output, input_grad, tile_grads.astype(F32))]
    another operation x6 -> x0, local copies, waits for them, and re-layouts: 12.2 us -> none
  transfers between devices with their start and end apart: 2 -> 2, of which waited for: 2 -> 2; matrix products, arithmetic and copies ran while one was open for 9% -> 1% of each run, Pallas kernels for 0% -> 0%
where the time goes in v1:
time: 217 us
  waiting for transfers between devices  181 us (83%)
  Pallas kernels  16.9 us (8%)
  between operations  14 us (6%)
  other arithmetic  4.1 us (2%)
    reduce_scatter x1, waiting for transfers between devices, on_device(): lax.psum_scatter(grads, 'fsdp', scatter_dimension=0, tiled=True)  103 us
    all_gather x1, waiting for transfers between devices, on_device(): gathered = lax.all_gather(tile_store, 'fsdp', axis=0, tiled=True)  77.1 us
    pallas_call x1, Pallas kernels, layer(): pl.pallas_call(layer_kernel, out_shape=(jax.ShapeDtypeStruct(x.shape, BF)...  16.9 us
  transfers between devices with their start and end apart: 2, of which 2 were waited for; matrix products, arithmetic and copies ran while one was open for 1% of the time, Pallas kernels for 0%

profile of v1, /device:TPU:0, one launch (start us, length us, event | category | flops | bytes accessed | tf_op | source)
XLA Modules:
  0.0 216.6 jit_solution(16272489704682300269)
XLA Ops:
  7.2 0.0 all-gather.2.cloned.1.call-start
  7.2 0.7 all-gather.2.cloned.1.call-update
  7.9 0.0 reduce-scatter.2.cloned.1.call-start
  7.9 0.8 fusion
  8.7 0.7 iota_reduce_fusion
  9.4 1.3 pad_add_fusion.idx
  10.7 77.1 %all-gather.2.cloned.1.call-done.store = bf16[256,128,128]{2,1,0:T(8,128)(2,1)} async-done(((bf16[16,128,128]{2,1,0:T(8,128)(2,1)}), bf16[256,128,128]{2,1,0:T(8,128)(2,1)}) %all-gather.2.cloned.1.call-update) | async-done | bytes 8388624 | tf_op jit(solution)/shard_map/all_gather | solution.py:137
  87.8 16.9 %shard_map.76 = (bf16[128,4096]{1,0:T(8,128)(2,1)}, bf16[128,4096]{1,0:T(8,128)(2,1)}, bf16[256,128,128]{2,1,0:T(8,128)(2,1)}) custom-call(s32[5,40]{1,0:T(8,128)} %pad_add_fusion.idx, bf16[128,4096]{1,0:T(8,128)(2,1)} %x.1, bf16[128,4096]{1,0:T(8,128)(2,1)} %c.1, bf16[256,128,128]{2,1,0:T(8,128)(2,1)} %all-gather.2.cloned.1.call-done.store), custom_call_target="tpu_custom_call" | custom-call | tf_op jit(solution)/shard_map/pallas_call | solution.py:109
  104.7 0.0 reduce-scatter.2.cloned.1.call-update
  104.7 103.0 %reduce-scatter.2.cloned.1.call-done = bf16[16,128,128]{2,1,0:T(8,128)(2,1)} async-done(((bf16[256,128,128]{2,1,0:T(8,128)(2,1)}), bf16[16,128,128]{2,1,0:T(8,128)(2,1)}) %reduce-scatter.2.cloned.1.call-update) | async-done | bytes 524304 | tf_op jit(solution)/shard_map/reduce_scatter | solution.py:139
  207.7 2.1 convert_element_type.3
Async XLA Ops:
  7.2 80.6 %all-gather.2.cloned.1.call-start = ((), (), s32[]{:S(2)}) async-start(), calls=%async_computation.1 | async-start | bytes 8912896 | tf_op jit(solution)/shard_map/all_gather | solution.py:137
  7.9 199.8 %reduce-scatter.2.cloned.1.call-start = ((), (), s32[]{:S(2)}) async-start(), calls=%async_computation.2 | async-start | bytes 8912896 | tf_op jit(solution)/shard_map/reduce_scatter | solution.py:139
Sparse Core Ops, SparseCore 0:
  10.2 77.5 all-gather.1
  104.8 102.8 reduce-scatter.1

commit v2 on v1

--- a/solution.py
+++ b/solution.py
@@ -1,3 +1,5 @@
+import functools
+
 import jax
 import jax.numpy as jnp
 from jax import lax
@@ -15,8 +17,8 @@
 
 
 def layer_kernel(
-    idx, x, c, store, out, xgrad, grads,
-    wgu, wd, gu, dh, hid, dgu, oacc, xacc, sems,
+    idx, x, c, store, out, xgrad, left, right,
+    wgu, wd, gu, dh, oacc, xacc, sems,
 ):
     tiles = wd.shape[0]
     side = wd.shape[1]
@@ -29,12 +31,6 @@
         return carry
 
     lax.fori_loop(0, tiles, fetch, 0)
-
-    def clear(s, carry):
-        grads[s] = jnp.zeros((side, side), BF)
-        return carry
-
-    lax.fori_loop(0, grads.shape[0], clear, 0, unroll=8)
 
     def clear_rows(s, carry):
         oacc[s] = jnp.zeros((side, side), F32)
@@ -69,9 +65,9 @@
             d = dh[j]
             sig = jax.nn.sigmoid(gate)
             act = gate * sig
-            hid[j] = (act * up).astype(BF)
-            dgu[j, :, :side] = (d * up * sig * (1.0 + gate * (1.0 - sig))).astype(BF)
-            dgu[j, :, side:] = (d * act).astype(BF)
+            left[row_blocks + j] = (act * up).astype(BF)
+            right[j] = (d * up * sig * (1.0 + gate * (1.0 - sig))).astype(BF)
+            right[tiles + j] = (d * act).astype(BF)
 
         return carry
 
@@ -80,22 +76,19 @@
     def backward(j, carry):
         a = idx[0, j]
         k = idx[1, j]
-        h = hid[k]
-        d2 = dgu[k]
-        xj = block(x, j)
-        cj = block(c, j)
+        h = left[row_blocks + k]
+        d2 = jnp.concatenate([right[k], right[tiles + k]], axis=1)
         w2 = jnp.concatenate([wgu[0, j], wgu[1, j]], axis=1)
         oacc[a] += dot(h, wd[j], 1, 0)
         xacc[a] += dot(d2, w2, 1, 1)
-        g2 = dot(xj, d2, 0, 0).astype(BF)
-        grads[idx[2, j]] = g2[:, :side]
-        grads[idx[3, j]] = g2[:, side:]
-        grads[idx[4, j]] = dot(h, cj, 0, 0).astype(BF)
         return carry
 
     lax.fori_loop(0, tiles, backward, 0, unroll=4)
 
+    left[row_blocks + tiles] = jnp.zeros((x.shape[0], side), BF)
     for s in range(row_blocks):
+        left[s] = x[:, s * side:(s + 1) * side]
+        right[2 * tiles + s] = c[:, s * side:(s + 1) * side]
         out[:, s * side:(s + 1) * side] = oacc[s].astype(BF)
         xgrad[:, s * side:(s + 1) * side] = xacc[s].astype(BF)
 
@@ -111,17 +104,16 @@
         out_shape=(
             jax.ShapeDtypeStruct(x.shape, BF),
             jax.ShapeDtypeStruct(x.shape, BF),
-            jax.ShapeDtypeStruct(store.shape, BF),
+            jax.ShapeDtypeStruct((row_blocks + tiles + 1, n_rows, side), BF),
+            jax.ShapeDtypeStruct((2 * tiles + row_blocks, n_rows, side), BF),
         ),
         in_specs=[pl.BlockSpec(memory_space=pltpu.SMEM), vmem, vmem, pl.BlockSpec(memory_space=pl.ANY)],
-        out_specs=(vmem, vmem, vmem),
+        out_specs=(vmem, vmem, vmem, vmem),
         scratch_shapes=[
             pltpu.VMEM((2, tiles, side, side), BF),
             pltpu.VMEM((tiles, side, side), BF),
             pltpu.VMEM((tiles, n_rows, 2 * side), F32),
             pltpu.VMEM((tiles, n_rows, side), F32),
-            pltpu.VMEM((tiles, n_rows, side), BF),
-            pltpu.VMEM((tiles, n_rows, 2 * side), BF),
             pltpu.VMEM((row_blocks, n_rows, side), F32),
             pltpu.VMEM((row_blocks, n_rows, side), F32),
             pltpu.SemaphoreType.DMA((2,)),
@@ -130,14 +122,403 @@
     )(idx, x, c, store)
 
 
-def on_device(inputs, cotangent, tile_store, pattern, tile_slot):
+def place():
+    me = lax.axis_index("fsdp")
+    return me // 4, lax.rem(me // 2, 2), lax.rem(me, 2)
+
+
+def at(z, y, c):
+    return (z * 2 + y) * 2 + c
+
+
+def greet(partners):
+    barrier = pltpu.get_barrier_semaphore()
+    for ok, dev in partners:
+        if ok is None:
+            pl.semaphore_signal(barrier, inc=1, device_id=dev, device_id_type=pl.DeviceIdType.MESH)
+        else:
+            @pl.when(ok)
+            def _():
+                pl.semaphore_signal(barrier, inc=1, device_id=dev, device_id_type=pl.DeviceIdType.MESH)
+    count = sum(1 if ok is None else ok.astype(jnp.int32) for ok, _ in partners)
+    pl.semaphore_wait(barrier, count)
+
+
+def remote(src, dst, send_sem, recv_sem, dev):
+    return pltpu.make_async_remote_copy(
+        src_ref=src, dst_ref=dst, send_sem=send_sem, recv_sem=recv_sem,
+        device_id=dev, device_id_type=pl.DeviceIdType.MESH,
+    )
+
+
+N_CHUNK = 8
+N_BOTH = 2
+N_HALF = 3
+
+
+def gather_kernel(store, full, local_sem, send_sem, recv_sem):
+    z, y, c = place()
+    g = lax.axis_index("groups")
+    cap = store.shape[0]
+    size = cap // N_CHUNK
+    dev_up = {"fsdp": at(z + 1, y, c)}
+    dev_down = {"fsdp": at(z - 1, y, c)}
+    dev_y = {"fsdp": at(z, 1 - y, c)}
+    dev_x = {"groups": 1 - g}
+    dev_core = {"fsdp": at(z, y, 1 - c)}
+    greet([(z < 3, dev_up), (z > 0, dev_down), (None, dev_y), (None, dev_x), (None, dev_core)])
+
+    def rows(owner, k):
+        return full.at[pl.ds(owner * cap + k * size, size)]
+
+    def copy(way, dev, owner, k, src=None):
+        dst = rows(owner, k)
+        return remote(dst if src is None else src, dst, send_sem.at[way, owner // 2, k], recv_sem.at[owner, k], dev)
+
+    def send(way, dev, owner, k, act, src=None):
+        d = copy(way, dev, owner, k, src)
+        d.start() if act else d.wait_send()
+
+    def chunk(i):
+        return jnp.where(i < N_BOTH, i, i + g * N_HALF)
+
+    def other(i):
+        return N_BOTH + (1 - g) * N_HALF + i
+
+    own = at(z, y, c)
+    keep = pltpu.make_async_copy(store, full.at[pl.ds(own * cap, cap)], local_sem)
+
+    def own_sends(act):
+        def body(i, carry):
+            k = chunk(i)
+            src = store.at[pl.ds(k * size, size)]
+
+            @pl.when(z < 3)
+            def _():
+                send(0, dev_up, own, k, act, src)
+
+            @pl.when(z > 0)
+            def _():
+                send(1, dev_down, own, k, act, src)
+
+            send(2, dev_y, own, k, act, src)
+            return carry
+
+        lax.fori_loop(0, N_BOTH + N_HALF, body, 0)
+
+        def body_core(k, carry):
+            send(4, dev_core, own, k, act, store.at[pl.ds(k * size, size)])
+            return carry
+
+        lax.fori_loop(0, N_CHUNK, body_core, 0)
+
+    def line(d, act):
+        def body(i, carry):
+            k = chunk(i)
+            for below in (True, False):
+                src_z = z - d if below else z + d
+                owner = at(src_z, y, c)
+
+                @pl.when((src_z >= 0) if below else (src_z <= 3))
+                def _():
+                    if act:
+                        copy(0, dev_core, owner, k).wait_recv()
+
+                    @pl.when((z < 3) if below else (z > 0))
+                    def _():
+                        if below:
+                            send(0, dev_up, owner, k, act)
+                        else:
+                            send(1, dev_down, owner, k, act)
+
+                    send(2, dev_y, owner, k, act)
+
+                    @pl.when(i >= N_BOTH)
+                    def _():
+                        send(3, dev_x, owner, k, act)
+
+                    send(4, dev_core, owner, k, act)
+
+            return carry
+
+        lax.fori_loop(0, N_BOTH + N_HALF, body, 0)
+
+    def across_y(d, act):
+        def body(i, carry):
+            k = chunk(i)
+            for src_z in ((z,) if d == 0 else (z - d, z + d)):
+                owner = at(src_z, 1 - y, c)
+
+                @pl.when((src_z >= 0) & (src_z <= 3))
+                def _():
+                    if act:
+                        copy(0, dev_core, owner, k).wait_recv()
+
+                    @pl.when(i >= N_BOTH)
+                    def _():
+                        send(3, dev_x, owner, k, act)
+
+                    send(4, dev_core, owner, k, act)
+
+            return carry
+
+        lax.fori_loop(0, N_BOTH + N_HALF, body, 0)
+
+    def across_x(d, act):
+        def body(i, carry):
+            k = other(i)
+            for src_z in ((z,) if d == 0 else (z - d, z + d)):
+                for yy in ((1 - y,) if d == 0 else (y, 1 - y)):
+                    owner = at(src_z, yy, c)
+
+                    @pl.when((src_z >= 0) & (src_z <= 3))
+                    def _():
+                        if act:
+                            copy(0, dev_core, owner, k).wait_recv()
+                        send(4, dev_core, owner, k, act)
+
+            return carry
+
+        lax.fori_loop(0, N_HALF, body, 0)
+
+    own_sends(True)
+    keep.start()
+    steps = ((line, 1), (across_y, 0), (line, 2), (across_y, 1), (across_x, 0), (line, 3), (across_x, 1),
+             (across_y, 2), (across_x, 2), (across_y, 3), (across_x, 3))
+    for step, d in steps:
+        step(d, True)
+
+    def core_in(i, carry):
+        owner = (i // N_CHUNK) * 2 + 1 - c
+        copy(0, dev_core, owner, lax.rem(i, N_CHUNK)).wait_recv()
+        return carry
+
+    lax.fori_loop(0, 8 * N_CHUNK, core_in, 0)
+    keep.wait()
+    own_sends(False)
+    for step, d in steps:
+        step(d, False)
+
+
+def gather_tiles(store):
+    cap, side, _ = store.shape
+    return pl.pallas_call(
+        gather_kernel,
+        out_shape=jax.ShapeDtypeStruct((16 * cap, side, side), BF),
+        in_specs=[pl.BlockSpec(memory_space=pl.ANY)],
+        out_specs=pl.BlockSpec(memory_space=pl.ANY),
+        scratch_shapes=[
+            pltpu.SemaphoreType.DMA,
+            pltpu.SemaphoreType.DMA((5, 8, N_CHUNK)),
+            pltpu.SemaphoreType.DMA((16, N_CHUNK)),
+        ],
+        compiler_params=pltpu.CompilerParams(collective_id=0, has_side_effects=True),
+    )(store)
+
+
+def scatter_kernel(
+    lidx, ridx, left, right, out, part, core_in, y_in, lo_in, hi_in,
+    core_s, core_r, y_s, y_r, z_s, lo_r, hi_r,
+):
+    z, y, c = place()
+    cap = out.shape[0]
+    dev_up = {"fsdp": at(z + 1, y, c)}
+    dev_down = {"fsdp": at(z - 1, y, c)}
+    dev_y = {"fsdp": at(z, 1 - y, c)}
+    dev_core = {"fsdp": at(z, y, 1 - c)}
+    greet([(z < 3, dev_up), (z > 0, dev_down), (None, dev_y), (None, dev_core)])
+
+    def order(t):
+        base = jnp.where((z == 0) | (z == 3), 3 - t, (3, 0, 2, 1)[t])
+        return jnp.where(z >= 2, 3 - base, base)
+
+    def compute(owner):
+        def body(i, carry):
+            s = owner * cap + i
+            part[s] = dot(left[lidx[s]], right[ridx[s]], 0, 0).astype(BF)
+            return carry
+
+        lax.fori_loop(0, cap, body, 0, unroll=4)
+
+    def mine(owner):
+        return part.at[pl.ds(owner * cap, cap)]
+
+    def core_copy(o, yy):
+        return remote(mine(at(o, yy, 1 - c)), core_in.at[o * 2 + yy], core_s.at[o * 2 + yy], core_r.at[o * 2 + yy], dev_core)
+
+    def y_copy(o):
+        return remote(mine(at(o, 1 - y, c)), y_in.at[o], y_s.at[o], y_r.at[o], dev_y)
+
+    def up_copy(o):
+        return remote(mine(at(o, y, c)), lo_in.at[o], z_s.at[o], lo_r.at[o], dev_up)
+
+    def down_copy(o):
+        return remote(mine(at(o, y, c)), hi_in.at[o], z_s.at[o], hi_r.at[o], dev_down)
+
+    def add(owner, terms, final=False):
+        def body(i, carry):
+            s = owner * cap + i
+            total = part[s].astype(F32)
+            for ref, slot in terms:
+                total += ref[slot, i].astype(F32)
+            if final:
+                out[i] = total
+            else:
+                part[s] = total.astype(BF)
+            return carry
+
+        lax.fori_loop(0, cap, body, 0, unroll=2)
+
+    for t in range(4):
+        o = order(t)
+        compute(at(o, 1 - y, 1 - c))
+        core_copy(o, 1 - y).start()
+    for t in range(4):
+        o = order(t)
+        compute(at(o, 1 - y, c))
+        core_copy(o, 1 - y).wait_recv()
+        add(at(o, 1 - y, c), [(core_in, o * 2 + 1 - y)])
+        y_copy(o).start()
+    for t in range(4):
+        o = order(t)
+        compute(at(o, y, 1 - c))
+        core_copy(o, y).start()
+    for t in range(4):
+        compute(at(order(t), y, c))
+    for t in range(4):
+        o = order(t)
+        owner = at(o, y, c)
+        core_copy(o, y).wait_recv()
+        y_copy(o).wait_recv()
+        terms = [(core_in, o * 2 + y), (y_in, o)]
+        if t < 3:
+            @pl.when(o < z)
+            def _():
+                @pl.when(z < 3)
+                def _():
+                    down_copy(o).wait_recv()
+                    add(owner, terms + [(hi_in, o)])
+
+                @pl.when(z == 3)
+                def _():
+                    add(owner, terms)
+
+                down_copy(o).start()
+
+            @pl.when(o > z)
+            def _():
+                @pl.when(z > 0)
+                def _():
+                    up_copy(o).wait_recv()
+                    add(owner, terms + [(lo_in, o)])
+
+                @pl.when(z == 0)
+                def _():
+                    add(owner, terms)
+
+                up_copy(o).start()
+        else:
+            @pl.when(z < 3)
+            def _():
+                down_copy(o).wait_recv()
+
+            @pl.when(z > 0)
+            def _():
+                up_copy(o).wait_recv()
+
+            @pl.when(z == 0)
+            def _():
+                add(owner, terms + [(hi_in, o)], True)
+
+            @pl.when(z == 3)
+            def _():
+                add(owner, terms + [(lo_in, o)], True)
+
+            @pl.when((z > 0) & (z < 3))
+            def _():
+                add(owner, terms + [(hi_in, o), (lo_in, o)], True)
+
+    for t in range(4):
+        o = order(t)
+        core_copy(o, y).wait_send()
+        core_copy(o, 1 - y).wait_send()
+        y_copy(o).wait_send()
+        if t < 3:
+            up_copy(o).wait_send()
+
+
+def scatter_grads(lidx, ridx, left, right):
+    slots = lidx.shape[0]
+    cap = slots // 16
+    side = left.shape[2]
+    vmem = pl.BlockSpec(memory_space=pltpu.VMEM)
+    smem = pl.BlockSpec(memory_space=pltpu.SMEM)
+    dma = pltpu.SemaphoreType.DMA
+    return pl.pallas_call(
+        scatter_kernel,
+        out_shape=jax.ShapeDtypeStruct((cap, side, side), F32),
+        in_specs=[smem, smem, vmem, vmem],
+        out_specs=vmem,
+        scratch_shapes=[
+            pltpu.VMEM((slots, side, side), BF),
+            pltpu.VMEM((8, cap, side, side), BF),
+            pltpu.VMEM((4, cap, side, side), BF),
+            pltpu.VMEM((4, cap, side, side), BF),
+            pltpu.VMEM((4, cap, side, side), BF),
+            dma((8,)), dma((8,)), dma((4,)), dma((4,)), dma((4,)), dma((4,)), dma((4,)),
+        ],
+        compiler_params=pltpu.CompilerParams(
+            collective_id=1, has_side_effects=True, vmem_limit_bytes=VMEM_BYTES
+        ),
+    )(lidx, ridx, left, right)
+
+
+def grads_kernel(lidx, ridx, left, right, grads):
+    def body(s, carry):
+        grads[s] = dot(left[lidx[s]], right[ridx[s]], 0, 0).astype(BF)
+        return carry
+
+    lax.fori_loop(0, grads.shape[0], body, 0, unroll=4)
+
+
+def local_grads(lidx, ridx, left, right):
+    vmem = pl.BlockSpec(memory_space=pltpu.VMEM)
+    smem = pl.BlockSpec(memory_space=pltpu.SMEM)
+    side = left.shape[2]
+    return pl.pallas_call(
+        grads_kernel,
+        out_shape=jax.ShapeDtypeStruct((lidx.shape[0], side, side), BF),
+        in_specs=[smem, smem, vmem, vmem],
+        out_specs=vmem,
+        compiler_params=pltpu.CompilerParams(vmem_limit_bytes=VMEM_BYTES),
+    )(lidx, ridx, left, right)
+
+
+def on_device(on_grid, inputs, cotangent, tile_store, pattern, tile_slot):
+    tiles = pattern.shape[1]
+    row_blocks = inputs.shape[1] // tile_store.shape[1]
     cols = pattern[1]
     first = jnp.argmax(cols[:, None] == cols[None, :], axis=1).astype(jnp.int32)
     idx = jnp.concatenate([pattern[:1], first[None], tile_slot], axis=0)
-    gathered = lax.all_gather(tile_store, "fsdp", axis=0, tiled=True)
-    output, input_grad, grads = layer(idx, inputs, cotangent, gathered)
-    tile_grads = lax.psum_scatter(grads, "fsdp", scatter_dimension=0, tiled=True)
-    return output, input_grad, tile_grads.astype(F32)
+    slots = tile_store.shape[0] * lax.axis_size("fsdp")
+    rows = pattern[0]
+    empty = row_blocks + tiles
+    pick_l = jnp.concatenate([rows, rows, row_blocks + first]) - empty
+    pick_r = jnp.concatenate([first, tiles + first, 2 * tiles + rows])
+    hit = jnp.arange(slots, dtype=jnp.int32)[:, None] == tile_slot.reshape(1, -1)
+    lidx = jnp.sum(jnp.where(hit, pick_l, 0), axis=1, dtype=jnp.int32) + empty
+    ridx = jnp.sum(jnp.where(hit, pick_r, 0), axis=1, dtype=jnp.int32)
+    if on_grid:
+        gathered = gather_tiles(tile_store)
+    else:
+        gathered = lax.all_gather(tile_store, "fsdp", axis=0, tiled=True)
+    output, input_grad, left, right = layer(idx, inputs, cotangent, gathered)
+    if on_grid:
+        tile_grads = scatter_grads(lidx, ridx, left, right)
+    else:
+        grads = local_grads(lidx, ridx, left, right)
+        tile_grads = lax.psum_scatter(grads, "fsdp", scatter_dimension=0, tiled=True).astype(F32)
+    return output, input_grad, tile_grads
 
 
 def solution(mesh):
@@ -148,8 +529,9 @@
         P(),
         P(),
     )
+    on_grid = mesh.shape["fsdp"] == 16 and mesh.shape["groups"] == 2
     return jax.shard_map(
-        on_device,
+        functools.partial(on_device, on_grid),
         mesh=mesh,
         in_specs=placed,
         out_specs=(

time: 217 us -> 134 us (0.62)
  the two profiles are of different devices: /device:TPU:0 before, /device:TPU:4 now
where the time goes in v2:
time: 134 us
  Pallas kernels  127 us (95%)
  other arithmetic  3.35 us (2%)
  local copies, waits for them, and re-layouts  3.15 us (2%)
    pallas_call x1, Pallas kernels, scatter_grads(): pl.pallas_call(scatter_kernel, out_shape=jax.ShapeDtypeStruct((cap, side,...  64.6 us
    pallas_call x1, Pallas kernels, gather_tiles(): pl.pallas_call(gather_kernel, out_shape=jax.ShapeDtypeStruct((16 * cap, s...  46.9 us
    pallas_call x1, Pallas kernels, layer(): pl.pallas_call(layer_kernel, out_shape=(jax.ShapeDtypeStruct(x.shape, BF)...  15 us

profile of v2, /device:TPU:4, one launch (start us, length us, event | category | flops | bytes accessed | tf_op | source)
XLA Modules:
  0.0 133.8 jit_solution(990150716895021952)
XLA Ops:
  0.6 0.8 slice_bitcast_fusion.1
  1.4 0.7 iota_reduce_fusion
  2.1 1.3 pad_add_fusion.idx
  3.4 46.9 %shard_map.76.store = bf16[256,128,128]{2,1,0:T(8,128)(2,1)} custom-call(bf16[16,128,128]{2,1,0:T(8,128)(2,1)} %store.1), custom_call_target="tpu_custom_call" | custom-call | tf_op jit(solution)/shard_map/pallas_call | solution.py:305
  50.3 0.0 copy-start.1
  50.3 0.0 copy-start
  50.3 15.0 %shard_map.77 = (bf16[128,4096]{1,0:T(8,128)(2,1)}, bf16[128,4096]{1,0:T(8,128)(2,1)}, bf16[73,128,128]{2,1,0:T(8,128)(2,1)}, bf16[112,128,128]{2,1,0:T(8,128)(2,1)}) custom-call(s32[5,40]{1,0:T(8,128)} %pad_add_fusion.idx, bf16[128,4096]{1,0:T(8,128)(2,1)} %x.1, bf16[128,4096]{1,0:T(8,128)(2,1)} %c.1, bf16[256,128,128]{2,1,0:T(8,128)(2,1)} %shard_map.76.store), custom_call_target="tpu_custom_call" | custom-call | tf_op jit(solution)/shard_map/pallas_call | solution.py:102
  65.4 0.0 copy-done.1
  65.4 0.1 add_add_fusion
  65.5 0.0 copy-done
  65.5 0.1 eq.37
  65.6 0.7 select_reduce_fusion
  66.3 0.6 broadcast_add_fusion.lidx
  66.9 64.6 %shard_map.78 = f32[16,128,128]{2,1,0:T(8,128)} custom-call(s32[256]{0:T(256)} %broadcast_add_fusion.lidx, s32[256]{0:T(256)} %get-tuple-element.13.ridx, bf16[73,128,128]{2,1,0:T(8,128)(2,1)} %get-tuple-element.11.left, bf16[112,128,128]{2,1,0:T(8,128)(2,1)} %get-tuple-element.12.right), custom_call_target="tpu_custom_call" | custom-call | tf_op jit(solution)/shard_map/pallas_call | solution.py:457
  131.5 2.3 %copy.9 = f32[16,128,128]{2,1,0:T(8,128)} copy(f32[16,128,128]{2,1,0:T(8,128)} %shard_map.78) | data formatting | bytes 2097152
  (2 shorter events, 0.0 us)
Async XLA Ops:
  50.3 15.1 %copy-start.1 = (s32[2,40]{1,0:T(2,128)S(1)}, s32[2,40]{1,0:T(2,128)}, u32[]{:S(2)}) copy-start(s32[2,40]{1,0:T(2,128)} %param.8) | copy-start | bytes 964
  50.3 15.2 %copy-start = (s32[3,40]{1,0:T(4,128)S(1)}, s32[3,40]{1,0:T(4,128)}, u32[]{:S(2)}) copy-start(s32[3,40]{1,0:T(4,128)} %param.9) | copy-start | bytes 1444

commit v3 on v2

--- a/solution.py
+++ b/solution.py
@@ -9,6 +9,7 @@
 
 BF = jnp.bfloat16
 F32 = jnp.float32
+FF = 14336
 VMEM_BYTES = 56 * 1024 * 1024
 
 
@@ -17,20 +18,48 @@
 
 
 def layer_kernel(
-    idx, x, c, store, out, xgrad, left, right,
-    wgu, wd, gu, dh, oacc, xacc, sems,
+    pattern, slot, x, c, store, out, xgrad, left, right, lidx, ridx,
+    first, col_first, wgu, wd, gu, dh, oacc, xacc, sems,
 ):
     tiles = wd.shape[0]
     side = wd.shape[1]
     row_blocks = oacc.shape[0]
 
     def fetch(j, carry):
-        pltpu.make_async_copy(store.at[idx[2, j]], wgu.at[0, j], sems.at[0]).start()
-        pltpu.make_async_copy(store.at[idx[3, j]], wgu.at[1, j], sems.at[0]).start()
-        pltpu.make_async_copy(store.at[idx[4, j]], wd.at[j], sems.at[1]).start()
+        pltpu.make_async_copy(store.at[slot[0, j]], wgu.at[0, j], sems.at[0]).start()
+        pltpu.make_async_copy(store.at[slot[1, j]], wgu.at[1, j], sems.at[0]).start()
+        pltpu.make_async_copy(store.at[slot[2, j]], wd.at[j], sems.at[1]).start()
         return carry
 
     lax.fori_loop(0, tiles, fetch, 0)
+
+    def note_column(i, carry):
+        j = tiles - 1 - i
+        col_first[pattern[1, j]] = j
+        return carry
+
+    lax.fori_loop(0, tiles, note_column, 0, unroll=4)
+
+    def empty_slot(s, carry):
+        lidx[s] = row_blocks + tiles
+        ridx[s] = 0
+        return carry
+
+    lax.fori_loop(0, lidx.shape[0], empty_slot, 0, unroll=8)
+
+    def fill_slot(j, carry):
+        a = pattern[0, j]
+        k = col_first[pattern[1, j]]
+        first[j] = k
+        lidx[slot[0, j]] = a
+        ridx[slot[0, j]] = k
+        lidx[slot[1, j]] = a
+        ridx[slot[1, j]] = tiles + k
+        lidx[slot[2, j]] = row_blocks + k
+        ridx[slot[2, j]] = 2 * tiles + a
+        return carry
+
+    lax.fori_loop(0, tiles, fill_slot, 0, unroll=2)
 
     def clear_rows(s, carry):
         oacc[s] = jnp.zeros((side, side), F32)
@@ -42,10 +71,10 @@
     pltpu.make_async_copy(wd, wd, sems.at[1]).wait()
 
     def block(ref, j):
-        return ref[:, pl.ds(pl.multiple_of(idx[0, j] * side, side), side)]
+        return ref[:, pl.ds(pl.multiple_of(pattern[0, j] * side, side), side)]
 
     def forward(j, carry):
-        k = idx[1, j]
+        k = first[j]
         xj = block(x, j)
         w2 = jnp.concatenate([wgu[0, j], wgu[1, j]], axis=1)
         part = dot(xj, w2, 1, 0)
@@ -58,7 +87,7 @@
     lax.fori_loop(0, tiles, forward, 0, unroll=4)
 
     def gates(j, carry):
-        @pl.when(idx[1, j] == j)
+        @pl.when(first[j] == j)
         def _():
             gate = gu[j, :, :side]
             up = gu[j, :, side:]
@@ -74,8 +103,8 @@
     lax.fori_loop(0, tiles, gates, 0)
 
     def backward(j, carry):
-        a = idx[0, j]
-        k = idx[1, j]
+        a = pattern[0, j]
+        k = first[j]
         h = left[row_blocks + k]
         d2 = jnp.concatenate([right[k], right[tiles + k]], axis=1)
         w2 = jnp.concatenate([wgu[0, j], wgu[1, j]], axis=1)
@@ -93,11 +122,12 @@
         xgrad[:, s * side:(s + 1) * side] = xacc[s].astype(BF)
 
 
-def layer(idx, x, c, store):
+def layer(pattern, slot, x, c, store):
     n_rows, width = x.shape
     slots, side, _ = store.shape
-    tiles = idx.shape[1]
+    tiles = pattern.shape[1]
     row_blocks = width // side
+    smem = pl.BlockSpec(memory_space=pltpu.SMEM)
     vmem = pl.BlockSpec(memory_space=pltpu.VMEM)
     return pl.pallas_call(
         layer_kernel,
@@ -106,10 +136,14 @@
             jax.ShapeDtypeStruct(x.shape, BF),
             jax.ShapeDtypeStruct((row_blocks + tiles + 1, n_rows, side), BF),
             jax.ShapeDtypeStruct((2 * tiles + row_blocks, n_rows, side), BF),
+            jax.ShapeDtypeStruct((slots,), jnp.int32),
+            jax.ShapeDtypeStruct((slots,), jnp.int32),
         ),
-        in_specs=[pl.BlockSpec(memory_space=pltpu.SMEM), vmem, vmem, pl.BlockSpec(memory_space=pl.ANY)],
-        out_specs=(vmem, vmem, vmem, vmem),
+        in_specs=[smem, smem, vmem, vmem, pl.BlockSpec(memory_space=pl.ANY)],
+        out_specs=(vmem, vmem, vmem, vmem, smem, smem),
         scratch_shapes=[
+            pltpu.SMEM((tiles,), jnp.int32),
+            pltpu.SMEM((FF // side,), jnp.int32),
             pltpu.VMEM((2, tiles, side, side), BF),
             pltpu.VMEM((tiles, side, side), BF),
             pltpu.VMEM((tiles, n_rows, 2 * side), F32),
@@ -119,7 +153,7 @@
             pltpu.SemaphoreType.DMA((2,)),
         ],
         compiler_params=pltpu.CompilerParams(vmem_limit_bytes=VMEM_BYTES),
-    )(idx, x, c, store)
+    )(pattern, slot, x, c, store)
 
 
 def place():
@@ -151,12 +185,12 @@
     )
 
 
-N_CHUNK = 8
+N_CHUNK = 4
 N_BOTH = 2
-N_HALF = 3
-
-
-def gather_kernel(store, full, local_sem, send_sem, recv_sem):
+N_HALF = 1
+
+
+def gather_kernel(store, full, hold, local_sem, send_sem, recv_sem):
     z, y, c = place()
     g = lax.axis_index("groups")
     cap = store.shape[0]
@@ -180,13 +214,14 @@
         d.start() if act else d.wait_send()
 
     def chunk(i):
-        return jnp.where(i < N_BOTH, i, i + g * N_HALF)
+        return jnp.where(i < N_HALF, N_BOTH + g * N_HALF + i, i - N_HALF)
 
     def other(i):
         return N_BOTH + (1 - g) * N_HALF + i
 
     own = at(z, y, c)
-    keep = pltpu.make_async_copy(store, full.at[pl.ds(own * cap, cap)], local_sem)
+    load = pltpu.make_async_copy(store, hold, local_sem.at[0])
+    keep = pltpu.make_async_copy(hold, full.at[pl.ds(own * cap, cap)], local_sem.at[1])
 
     def own_sends(act):
         def body(i, carry):
@@ -233,7 +268,7 @@
 
                     send(2, dev_y, owner, k, act)
 
-                    @pl.when(i >= N_BOTH)
+                    @pl.when(i < N_HALF)
                     def _():
                         send(3, dev_x, owner, k, act)
 
@@ -254,7 +289,7 @@
                     if act:
                         copy(0, dev_core, owner, k).wait_recv()
 
-                    @pl.when(i >= N_BOTH)
+                    @pl.when(i < N_HALF)
                     def _():
                         send(3, dev_x, owner, k, act)
 
@@ -282,6 +317,8 @@
         lax.fori_loop(0, N_HALF, body, 0)
 
     own_sends(True)
+    load.start()
+    load.wait()
     keep.start()
     steps = ((line, 1), (across_y, 0), (line, 2), (across_y, 1), (across_x, 0), (line, 3), (across_x, 1),
              (across_y, 2), (across_x, 2), (across_y, 3), (across_x, 3))
@@ -308,7 +345,8 @@
         in_specs=[pl.BlockSpec(memory_space=pl.ANY)],
         out_specs=pl.BlockSpec(memory_space=pl.ANY),
         scratch_shapes=[
-            pltpu.SemaphoreType.DMA,
+            pltpu.VMEM(store.shape, BF),
+            pltpu.SemaphoreType.DMA((2,)),
             pltpu.SemaphoreType.DMA((5, 8, N_CHUNK)),
             pltpu.SemaphoreType.DMA((16, N_CHUNK)),
         ],
@@ -369,16 +407,21 @@
 
         lax.fori_loop(0, cap, body, 0, unroll=2)
 
-    for t in range(4):
-        o = order(t)
+    def to_core(o):
         compute(at(o, 1 - y, 1 - c))
         core_copy(o, 1 - y).start()
-    for t in range(4):
-        o = order(t)
+
+    def to_y(o):
         compute(at(o, 1 - y, c))
         core_copy(o, 1 - y).wait_recv()
         add(at(o, 1 - y, c), [(core_in, o * 2 + 1 - y)])
         y_copy(o).start()
+
+    to_core(order(0))
+    for t in range(4):
+        if t < 3:
+            to_core(order(t + 1))
+        to_y(order(t))
     for t in range(4):
         o = order(t)
         compute(at(o, y, 1 - c))
@@ -495,24 +538,11 @@
 
 
 def on_device(on_grid, inputs, cotangent, tile_store, pattern, tile_slot):
-    tiles = pattern.shape[1]
-    row_blocks = inputs.shape[1] // tile_store.shape[1]
-    cols = pattern[1]
-    first = jnp.argmax(cols[:, None] == cols[None, :], axis=1).astype(jnp.int32)
-    idx = jnp.concatenate([pattern[:1], first[None], tile_slot], axis=0)
-    slots = tile_store.shape[0] * lax.axis_size("fsdp")
-    rows = pattern[0]
-    empty = row_blocks + tiles
-    pick_l = jnp.concatenate([rows, rows, row_blocks + first]) - empty
-    pick_r = jnp.concatenate([first, tiles + first, 2 * tiles + rows])
-    hit = jnp.arange(slots, dtype=jnp.int32)[:, None] == tile_slot.reshape(1, -1)
-    lidx = jnp.sum(jnp.where(hit, pick_l, 0), axis=1, dtype=jnp.int32) + empty
-    ridx = jnp.sum(jnp.where(hit, pick_r, 0), axis=1, dtype=jnp.int32)
     if on_grid:
         gathered = gather_tiles(tile_store)
     else:
         gathered = lax.all_gather(tile_store, "fsdp", axis=0, tiled=True)
-    output, input_grad, left, right = layer(idx, inputs, cotangent, gathered)
+    output, input_grad, left, right, lidx, ridx = layer(pattern, tile_slot, inputs, cotangent, gathered)
     if on_grid:
         tile_grads = scatter_grads(lidx, ridx, left, right)
     else:

time: 134 us -> 122 us (0.910)
  the two profiles are of different devices: /device:TPU:4 before, /device:TPU:0 now
where the time goes in v3:
time: 122 us
  Pallas kernels  119 us (98%)
  local copies, waits for them, and re-layouts  2.3 us (2%)
    pallas_call x1, Pallas kernels, scatter_grads(): pl.pallas_call(scatter_kernel, out_shape=jax.ShapeDtypeStruct((cap, side,...  61.2 us
    pallas_call x1, Pallas kernels, gather_tiles(): pl.pallas_call(gather_kernel, out_shape=jax.ShapeDtypeStruct((16 * cap, s...  42.8 us
    pallas_call x1, Pallas kernels, layer(): pl.pallas_call(layer_kernel, out_shape=(jax.ShapeDtypeStruct(x.shape, BF)...  15 us

profile of v3, /device:TPU:0, one launch (start us, length us, event | category | flops | bytes accessed | tf_op | source)
XLA Modules:
  0.0 121.9 jit_solution(11452574793421432646)
XLA Ops:
  0.6 42.8 %shard_map.76.store = bf16[256,128,128]{2,1,0:T(8,128)(2,1)} custom-call(bf16[16,128,128]{2,1,0:T(8,128)(2,1)} %store.1), custom_call_target="tpu_custom_call" | custom-call | tf_op jit(solution)/shard_map/pallas_call | solution.py:342
  43.4 15.0 %shard_map.77 = (bf16[128,4096]{1,0:T(8,128)(2,1)}, bf16[128,4096]{1,0:T(8,128)(2,1)}, bf16[73,128,128]{2,1,0:T(8,128)(2,1)}, bf16[112,128,128]{2,1,0:T(8,128)(2,1)}, s32[256]{0:T(256)}, /*index=5*/s32[256]{0:T(256)}) custom-call(s32[2,40]{1,0:T(2,128)} %pattern.1, s32[3,40]{1,0:T(4,128)} %slot.1, bf16[128,4096]{1,0:T(8,128)(2,1)} %x.1, ...), custom_call_target="tpu_custom_call" | custom-call | tf_op jit(solution)/shard_map/pallas_call | solution.py:132
  58.4 61.2 %shard_map.78 = f32[16,128,128]{2,1,0:T(8,128)} custom-call(s32[256]{0:T(256)} %get-tuple-element.11.lidx, s32[256]{0:T(256)} %get-tuple-element.12.ridx, bf16[73,128,128]{2,1,0:T(8,128)(2,1)} %get-tuple-element.13.left, bf16[112,128,128]{2,1,0:T(8,128)(2,1)} %get-tuple-element.14.right), custom_call_target="tpu_custom_call" | custom-call | tf_op jit(solution)/shard_map/pallas_call | solution.py:500
  119.6 2.3 %copy.9 = f32[16,128,128]{2,1,0:T(8,128)} copy(f32[16,128,128]{2,1,0:T(8,128)} %shard_map.78) | data formatting | bytes 2097152

commit v4 on v3

--- a/solution.py
+++ b/solution.py
@@ -355,11 +355,12 @@
 
 
 def scatter_kernel(
-    lidx, ridx, left, right, out, part, core_in, y_in, lo_in, hi_in,
-    core_s, core_r, y_s, y_r, z_s, lo_r, hi_r,
+    lidx, ridx, left, right, out, part, core_in, y_in, lo_in, hi_in, far_lo, far_hi, far_y,
+    core_s, core_r, y_s, y_r, z_s, lo_r, hi_r, far_s, far_lo_r, far_hi_r, far_y_sem,
 ):
     z, y, c = place()
     cap = out.shape[0]
+    few = far_y.shape[0]
     dev_up = {"fsdp": at(z + 1, y, c)}
     dev_down = {"fsdp": at(z - 1, y, c)}
     dev_y = {"fsdp": at(z, 1 - y, c)}
@@ -385,7 +386,8 @@
         return remote(mine(at(o, yy, 1 - c)), core_in.at[o * 2 + yy], core_s.at[o * 2 + yy], core_r.at[o * 2 + yy], dev_core)
 
     def y_copy(o):
-        return remote(mine(at(o, 1 - y, c)), y_in.at[o], y_s.at[o], y_r.at[o], dev_y)
+        rest = pl.ds(at(o, 1 - y, c) * cap + few, cap - few)
+        return remote(part.at[rest], y_in.at[o, pl.ds(few, cap - few)], y_s.at[o], y_r.at[o], dev_y)
 
     def up_copy(o):
         return remote(mine(at(o, y, c)), lo_in.at[o], z_s.at[o], lo_r.at[o], dev_up)
@@ -393,19 +395,79 @@
     def down_copy(o):
         return remote(mine(at(o, y, c)), hi_in.at[o], z_s.at[o], hi_r.at[o], dev_down)
 
-    def add(owner, terms, final=False):
+    def far_rows(o):
+        return part.at[pl.ds(at(o, 1 - y, c) * cap, few)]
+
+    def far_up(o):
+        return remote(far_rows(o), far_lo.at[o], far_s.at[o], far_lo_r.at[o], dev_up)
+
+    def far_down(o):
+        return remote(far_rows(o), far_hi.at[o], far_s.at[o], far_hi_r.at[o], dev_down)
+
+    def far_y_copy():
+        return remote(far_rows(z), far_y, far_y_sem.at[0], far_y_sem.at[1], dev_y)
+
+    def add(owner, terms, start, stop, final=False):
         def body(i, carry):
             s = owner * cap + i
             total = part[s].astype(F32)
-            for ref, slot in terms:
-                total += ref[slot, i].astype(F32)
+            for get in terms:
+                total += get(i).astype(F32)
             if final:
                 out[i] = total
             else:
                 part[s] = total.astype(BF)
             return carry
 
-        lax.fori_loop(0, cap, body, 0, unroll=2)
+        lax.fori_loop(start, stop, body, 0, unroll=2)
+
+    def chain(t, o, up, down, lo, hi, total):
+        if t < 3:
+            @pl.when(o < z)
+            def _():
+                @pl.when(z < 3)
+                def _():
+                    down(o).wait_recv()
+                    total([lambda i: hi[o, i]])
+
+                @pl.when(z == 3)
+                def _():
+                    total([])
+
+                down(o).start()
+
+            @pl.when(o > z)
+            def _():
+                @pl.when(z > 0)
+                def _():
+                    up(o).wait_recv()
+                    total([lambda i: lo[o, i]])
+
+                @pl.when(z == 0)
+                def _():
+                    total([])
+
+                up(o).start()
+        else:
+            @pl.when(z < 3)
+            def _():
+                down(o).wait_recv()
+
+            @pl.when(z > 0)
+            def _():
+                up(o).wait_recv()
+
+            @pl.when(z == 0)
+            def _():
+                total([lambda i: hi[o, i]])
+
+            @pl.when(z == 3)
+            def _():
+                total([lambda i: lo[o, i]])
+
+            @pl.when((z > 0) & (z < 3))
+            def _():
+                total([lambda i: hi[o, i], lambda i: lo[o, i]])
 
     def to_core(o):
         compute(at(o, 1 - y, 1 - c))
@@ -414,7 +476,7 @@
     def to_y(o):
         compute(at(o, 1 - y, c))
         core_copy(o, 1 - y).wait_recv()
-        add(at(o, 1 - y, c), [(core_in, o * 2 + 1 - y)])
+        add(at(o, 1 - y, c), [lambda i: core_in[o * 2 + 1 - y, i]], few, cap)
         y_copy(o).start()
 
     to_core(order(0))
@@ -428,59 +490,31 @@
         core_copy(o, y).start()
     for t in range(4):
         compute(at(order(t), y, c))
-    for t in range(4):
-        o = order(t)
-        owner = at(o, y, c)
+    def far_step(t, o):
+        def total(terms):
+            add(at(o, 1 - y, c), [lambda i: core_in[o * 2 + 1 - y, i]] + terms, 0, few)
+
+        chain(t, o, far_up, far_down, far_lo, far_hi, total)
+
+    def near_step(t, o):
+        final = t == 3
         core_copy(o, y).wait_recv()
         y_copy(o).wait_recv()
-        terms = [(core_in, o * 2 + y), (y_in, o)]
-        if t < 3:
-            @pl.when(o < z)
-            def _():
-                @pl.when(z < 3)
-                def _():
-                    down_copy(o).wait_recv()
-                    add(owner, terms + [(hi_in, o)])
-
-                @pl.when(z == 3)
-                def _():
-                    add(owner, terms)
-
-                down_copy(o).start()
-
-            @pl.when(o > z)
-            def _():
-                @pl.when(z > 0)
-                def _():
-                    up_copy(o).wait_recv()
-                    add(owner, terms + [(lo_in, o)])
-
-                @pl.when(z == 0)
-                def _():
-                    add(owner, terms)
-
-                up_copy(o).start()
-        else:
-            @pl.when(z < 3)
-            def _():
-                down_copy(o).wait_recv()
-
-            @pl.when(z > 0)
-            def _():
-                up_copy(o).wait_recv()
-
-            @pl.when(z == 0)
-            def _():
-                add(owner, terms + [(hi_in, o)], True)
-
-            @pl.when(z == 3)
-            def _():
-                add(owner, terms + [(lo_in, o)], True)
-
-            @pl.when((z > 0) & (z < 3))
-            def _():
-                add(owner, terms + [(hi_in, o), (lo_in, o)], True)
-
+        if final:
+            far_y_copy().wait_recv()
+
+        def total(terms):
+            terms = [lambda i: core_in[o * 2 + y, i]] + terms
+            add(at(o, y, c), terms + ([lambda i: far_y[i]] if final else []), 0, few, final)
+            add(at(o, y, c), terms + [lambda i: y_in[o, i]], few, cap, final)
+
+        chain(t, o, up_copy, down_copy, lo_in, hi_in, total)
+
+    for t in range(4):
+        far_step(t, order(t))
+    far_y_copy().start()
+    for t in range(4):
+        near_step(t, order(t))
     for t in range(4):
         o = order(t)
         core_copy(o, y).wait_send()
@@ -488,11 +522,14 @@
         y_copy(o).wait_send()
         if t < 3:
             up_copy(o).wait_send()
+            far_up(o).wait_send()
+    far_y_copy().wait_send()
 
 
 def scatter_grads(lidx, ridx, left, right):
     slots = lidx.shape[0]
     cap = slots // 16
+    few = 3 * cap // 16
     side = left.shape[2]
     vmem = pl.BlockSpec(memory_space=pltpu.VMEM)
     smem = pl.BlockSpec(memory_space=pltpu.SMEM)
@@ -508,7 +545,11 @@
             pltpu.VMEM((4, cap, side, side), BF),
             pltpu.VMEM((4, cap, side, side), BF),
             pltpu.VMEM((4, cap, side, side), BF),
+            pltpu.VMEM((4, few, side, side), BF),
+            pltpu.VMEM((4, few, side, side), BF),
+            pltpu.VMEM((few, side, side), BF),
             dma((8,)), dma((8,)), dma((4,)), dma((4,)), dma((4,)), dma((4,)), dma((4,)),
+            dma((4,)), dma((4,)), dma((4,)), dma((2,)),
         ],
         compiler_params=pltpu.CompilerParams(
             collective_id=1, has_side_effects=True, vmem_limit_bytes=VMEM_BYTES

time: 122 us -> 127 us (1.041)
  Pallas kernels: 119 us -> 124 us
    pallas_call x1, Pallas kernels: 61.2 us -> 66.1 us  [scatter_grads(): pl.pallas_call(scatter_kernel, out_shape=jax.ShapeDtypeStruct((cap, side,...]
where the time goes in v4:
time: 127 us
  Pallas kernels  124 us (98%)
  local copies, waits for them, and re-layouts  2.3 us (2%)
    pallas_call x1, Pallas kernels, scatter_grads(): pl.pallas_call(scatter_kernel, out_shape=jax.ShapeDtypeStruct((cap, side,...  66.1 us
    pallas_call x1, Pallas kernels, gather_tiles(): pl.pallas_call(gather_kernel, out_shape=jax.ShapeDtypeStruct((16 * cap, s...  42.8 us
    pallas_call x1, Pallas kernels, layer(): pl.pallas_call(layer_kernel, out_shape=(jax.ShapeDtypeStruct(x.shape, BF)...  14.9 us

profile of v4, /device:TPU:0, one launch (start us, length us, event | category | flops | bytes accessed | tf_op | source)
XLA Modules:
  0.0 126.7 jit_solution(6793503520404786490)
XLA Ops:
  0.6 42.8 %shard_map.76.store = bf16[256,128,128]{2,1,0:T(8,128)(2,1)} custom-call(bf16[16,128,128]{2,1,0:T(8,128)(2,1)} %store.1), custom_call_target="tpu_custom_call" | custom-call | tf_op jit(solution)/shard_map/pallas_call | solution.py:342
  43.4 14.9 %shard_map.77 = (bf16[128,4096]{1,0:T(8,128)(2,1)}, bf16[128,4096]{1,0:T(8,128)(2,1)}, bf16[73,128,128]{2,1,0:T(8,128)(2,1)}, bf16[112,128,128]{2,1,0:T(8,128)(2,1)}, s32[256]{0:T(256)}, /*index=5*/s32[256]{0:T(256)}) custom-call(s32[2,40]{1,0:T(2,128)} %pattern.1, s32[3,40]{1,0:T(4,128)} %slot.1, bf16[128,4096]{1,0:T(8,128)(2,1)} %x.1, ...), custom_call_target="tpu_custom_call" | custom-call | tf_op jit(solution)/shard_map/pallas_call | solution.py:132
  58.3 66.1 %shard_map.78 = f32[16,128,128]{2,1,0:T(8,128)} custom-call(s32[256]{0:T(256)} %get-tuple-element.11.lidx, s32[256]{0:T(256)} %get-tuple-element.12.ridx, bf16[73,128,128]{2,1,0:T(8,128)(2,1)} %get-tuple-element.13.left, bf16[112,128,128]{2,1,0:T(8,128)(2,1)} %get-tuple-element.14.right), custom_call_target="tpu_custom_call" | custom-call | tf_op jit(solution)/shard_map/pallas_call | solution.py:537
  124.4 2.3 %copy.9 = f32[16,128,128]{2,1,0:T(8,128)} copy(f32[16,128,128]{2,1,0:T(8,128)} %shard_map.78) | data formatting | bytes 2097152

commit v5 on v4

--- a/solution.py
+++ b/solution.py
@@ -479,23 +479,27 @@
         add(at(o, 1 - y, c), [lambda i: core_in[o * 2 + 1 - y, i]], few, cap)
         y_copy(o).start()
 
+    def far_step(t, o):
+        def total(terms):
+            add(at(o, 1 - y, c), [lambda i: core_in[o * 2 + 1 - y, i]] + terms, 0, few)
+
+        chain(t, o, far_up, far_down, far_lo, far_hi, total)
+
     to_core(order(0))
     for t in range(4):
         if t < 3:
             to_core(order(t + 1))
         to_y(order(t))
+        if t > 0:
+            far_step(t - 1, order(t - 1))
     for t in range(4):
         o = order(t)
         compute(at(o, y, 1 - c))
         core_copy(o, y).start()
+    far_step(3, order(3))
+    far_y_copy().start()
     for t in range(4):
         compute(at(order(t), y, c))
-    def far_step(t, o):
-        def total(terms):
-            add(at(o, 1 - y, c), [lambda i: core_in[o * 2 + 1 - y, i]] + terms, 0, few)
-
-        chain(t, o, far_up, far_down, far_lo, far_hi, total)
-
     def near_step(t, o):
         final = t == 3
         core_copy(o, y).wait_recv()
@@ -510,9 +514,6 @@
 
         chain(t, o, up_copy, down_copy, lo_in, hi_in, total)
 
-    for t in range(4):
-        far_step(t, order(t))
-    far_y_copy().start()
     for t in range(4):
         near_step(t, order(t))
     for t in range(4):

time: 127 us -> 121 us (0.953)
  Pallas kernels: 124 us -> 117 us
    pallas_call x1, Pallas kernels: 66.1 us -> 59.8 us  [scatter_grads(): pl.pallas_call(scatter_kernel, out_shape=jax.ShapeDtypeStruct((cap, side,...]
where the time goes in v5:
time: 121 us; the launch traced here: 120 us
  Pallas kernels  117 us (97%)
  local copies, waits for them, and re-layouts  2.3 us (2%)
    pallas_call x1, Pallas kernels, scatter_grads(): pl.pallas_call(scatter_kernel, out_shape=jax.ShapeDtypeStruct((cap, side,...  59.8 us
    pallas_call x1, Pallas kernels, gather_tiles(): pl.pallas_call(gather_kernel, out_shape=jax.ShapeDtypeStruct((16 * cap, s...  42.8 us
    pallas_call x1, Pallas kernels, layer(): pl.pallas_call(layer_kernel, out_shape=(jax.ShapeDtypeStruct(x.shape, BF)...  14.8 us

profile of v5, /device:TPU:0, one launch (start us, length us, event | category | flops | bytes accessed | tf_op | source)
XLA Modules:
  0.0 120.3 jit_solution(10205499735288447791)
XLA Ops:
  0.6 42.8 %shard_map.76.store = bf16[256,128,128]{2,1,0:T(8,128)(2,1)} custom-call(bf16[16,128,128]{2,1,0:T(8,128)(2,1)} %store.1), custom_call_target="tpu_custom_call" | custom-call | tf_op jit(solution)/shard_map/pallas_call | solution.py:342
  43.4 14.8 %shard_map.77 = (bf16[128,4096]{1,0:T(8,128)(2,1)}, bf16[128,4096]{1,0:T(8,128)(2,1)}, bf16[73,128,128]{2,1,0:T(8,128)(2,1)}, bf16[112,128,128]{2,1,0:T(8,128)(2,1)}, s32[256]{0:T(256)}, /*index=5*/s32[256]{0:T(256)}) custom-call(s32[2,40]{1,0:T(2,128)} %pattern.1, s32[3,40]{1,0:T(4,128)} %slot.1, bf16[128,4096]{1,0:T(8,128)(2,1)} %x.1, ...), custom_call_target="tpu_custom_call" | custom-call | tf_op jit(solution)/shard_map/pallas_call | solution.py:132
  58.2 59.8 %shard_map.78 = f32[16,128,128]{2,1,0:T(8,128)} custom-call(s32[256]{0:T(256)} %get-tuple-element.11.lidx, s32[256]{0:T(256)} %get-tuple-element.12.ridx, bf16[73,128,128]{2,1,0:T(8,128)(2,1)} %get-tuple-element.13.left, bf16[112,128,128]{2,1,0:T(8,128)(2,1)} %get-tuple-element.14.right), custom_call_target="tpu_custom_call" | custom-call | tf_op jit(solution)/shard_map/pallas_call | solution.py:538
  118.0 2.3 %copy.9 = f32[16,128,128]{2,1,0:T(8,128)} copy(f32[16,128,128]{2,1,0:T(8,128)} %shard_map.78) | data formatting | bytes 2097152
